TPU v7x, 256 devices: a whole 4x4x8 slice. The times are simulated.
256 devices in a mesh: seq: 128 (over y, z, x_lo, core), chan: 2 (over x_hi).
Axes of the slice: x: 4 (x_hi: 2, x_lo: 2; x = x_hi * 2 + x_lo), y: 4, z: 8, core: 2. Of those that a mesh axis runs over, the one named last changes fastest.
Arguments:
- inputs: bfloat16 [262144, 256], P('seq', 'chan'), may hold values from -6 to 6
- cotangent: bfloat16 [262144, 256], P('seq', 'chan'), may hold values from -18 to 18
- residues: float32 [16, 16], replicated, may hold values from -4 to 4
- decay_rates: float32 [16, 16], replicated, may hold values from 1.9073486e-06 to 0.0333333333
- skip_weight: float32 [256], P('chan'), may hold values from -4 to 4
Outputs:
- input_grad: bfloat16 [262144, 256], P('seq', 'chan')
- residue_grad: float32 [16, 16], replicated
- skip_grad: float32 [256], P('chan')
All inputs are finite; a program needn't handle non-finite values.
Results may differ from a plain program's by a relative error of at most 0.0012.
Values may be sent and summed in bfloat16 or wider, within the bound.
A program may use at most 64 MiB of HBM per device.

v0:
```python
import math
import jax
import jax.numpy as jnp
from jax import lax
from jax.sharding import PartitionSpec as P

GROUP = 16
BLOCK = 512
NG = 16
precise = lax.Precision.HIGHEST


def join_states(earlier, later):
    return (earlier[0] * later[0], later[1] + later[0] * earlier[1])


def block_work(packed):
    x_item, y_item, powers, tail_powers, coef_item = packed
    block_len = x_item.shape[0]
    filter_taps = jnp.dot(coef_item, powers, precision=precise)
    padded = jnp.concatenate([filter_taps, jnp.zeros((block_len,), jnp.float32)])
    repeated = jnp.tile(padded, block_len)[: block_len * (2 * block_len - 1)]
    toeplitz = repeated.reshape(block_len, 2 * block_len - 1)[:, :block_len]
    x_float = x_item.astype(jnp.float32)
    y_float = y_item.astype(jnp.float32)
    local_dx = jnp.dot(toeplitz, y_float, precision=precise)
    gram_matrix = jnp.dot(x_float, y_float.T, precision=precise)
    widened = jnp.concatenate(
        [gram_matrix, jnp.zeros((block_len, block_len - 1), jnp.float32)], axis=1
    )
    flattened = jnp.concatenate([widened.reshape(-1), jnp.zeros((block_len,), jnp.float32)])
    lag_sums = jnp.sum(flattened.reshape(block_len, 2 * block_len)[:, :block_len], axis=0)
    local_grad = jnp.dot(powers, lag_sums, precision=precise)
    summaries = jnp.dot(powers, y_float, precision=precise)
    tails_x = jnp.dot(tail_powers, x_float, precision=precise)
    return (local_dx, local_grad, summaries, tails_x)


def convolve_items(x_items, y_items, rate_items, coef_items, block_count, incoming_fn):
    block_len = x_items.shape[1]
    offsets = jnp.arange(block_len, dtype=jnp.float32)
    powers = jnp.exp(-rate_items[:, :, None] * offsets)
    tail_powers = jnp.exp(-rate_items[:, :, None] * (block_len - offsets))
    local_dx, local_grad, summaries, tails_x = lax.map(
        block_work, (x_items, y_items, powers, tail_powers, coef_items)
    )
    item_count, mode_count, col_count = summaries.shape
    per_block = col_count // block_count
    states = summaries.reshape(item_count, mode_count, block_count, per_block)
    step_decay = jnp.exp(-rate_items * block_len)[:, :, None]
    ordered = jnp.flip(jnp.moveaxis(states, 2, 0), 0)
    factors = jnp.broadcast_to(step_decay, ordered.shape)
    inclusive = lax.associative_scan(join_states, (factors, ordered))[1]
    inclusive = jnp.moveaxis(jnp.flip(inclusive, 0), 0, 2)
    device_decay = jnp.exp(-rate_items * (block_len * block_count))[:, :, None]
    incoming = incoming_fn(device_decay, inclusive[:, :, 0])
    remaining = (block_count - 1 - jnp.arange(block_count)).astype(jnp.float32)
    reach_decay = jnp.exp(-rate_items[:, :, None] * (block_len * remaining))[..., None]
    after_state = jnp.concatenate(
        [inclusive[:, :, 1:], jnp.zeros_like(inclusive[:, :, :1])], axis=2
    )
    after_state = (after_state + reach_decay * incoming[:, :, None, :]).reshape(
        item_count, mode_count, col_count
    )
    cross_dx = jnp.einsum(
        "ims,imc->isc", coef_items[:, :, None] * tail_powers, after_state, precision=precise
    )
    cross_grad = jnp.sum(tails_x * after_state, axis=2)
    return (local_dx + cross_dx, local_grad + cross_grad)


def no_carry(device_decay, device_total):
    return jnp.zeros_like(device_total)


def shards(inputs, cotangent, residues, decay_rates, skip_weight):
    tokens, width_dev = inputs.shape
    total_len = tokens * lax.axis_size("seq")
    mode_norm = jnp.sqrt(-jnp.expm1(-2.0 * decay_rates))
    mode_coefs = residues * mode_norm
    skip_partial = jnp.einsum(
        "tc,tc->c", inputs, cotangent, preferred_element_type=jnp.float32
    ) / math.sqrt(total_len)
    x_wide, y_wide = (
        lax.all_to_all(inputs, "seq", split_axis=1, concat_axis=0, tiled=True),
        lax.all_to_all(cotangent, "seq", split_axis=1, concat_axis=0, tiled=True),
    )
    chan_dev = x_wide.shape[1]
    full_blocks = total_len // BLOCK
    x_items = jnp.transpose(x_wide.reshape(full_blocks, BLOCK, chan_dev), (2, 1, 0))
    y_items = jnp.transpose(y_wide.reshape(full_blocks, BLOCK, chan_dev), (2, 1, 0))
    first_channel = lax.axis_index("seq") * chan_dev
    channel_ids = first_channel + jnp.arange(chan_dev, dtype=jnp.int32)
    selector = (channel_ids[:, None] % NG == jnp.arange(NG, dtype=jnp.int32)[None, :]).astype(
        jnp.float32
    )
    rate_items = jnp.dot(selector, decay_rates, precision=precise)
    coef_items = jnp.dot(selector, mode_coefs, precision=precise)
    skip_items = lax.dynamic_slice_in_dim(skip_weight, first_channel, chan_dev)
    mixed, grads = convolve_items(x_items, y_items, rate_items, coef_items, full_blocks, no_carry)
    dx_items = (mixed + skip_items[:, None, None] * y_items.astype(jnp.float32)).astype(
        jnp.bfloat16
    )
    dx_wide = jnp.transpose(dx_items, (2, 1, 0)).reshape(total_len, chan_dev)
    input_grad = lax.all_to_all(dx_wide, "seq", split_axis=0, concat_axis=1, tiled=True)
    group_grad = jnp.dot(selector.T, grads, precision=precise) * mode_norm
    group_grad = group_grad / math.sqrt(GROUP * total_len)
    group_grad, skip_grad = lax.psum((group_grad, skip_partial), "seq")
    group_grad = lax.psum(group_grad, "chan")
    return (input_grad, group_grad, skip_grad)


def solution(mesh):
    placed = (P("seq", "chan"), P("seq", "chan"), P(), P(), P("chan"))
    return jax.shard_map(
        shards,
        mesh=mesh,
        in_specs=placed,
        out_specs=(P("seq", "chan"), P(), P("chan")),
        check_vma=False,
    )
```

profile of v0, /device:TPU:4, one launch (start us, length us, event | category | flops | bytes accessed | tf_op | source)
XLA Modules:
  0.0 402.8 jit_solution(14199440599802911040)
XLA Ops:
  0.6 2.5 copy.48
  3.1 0.5 broadcast.329
  3.7 3.7 reduce.8
  7.3 1.2 reshape.387
  8.5 14.4 %all-to-all-start = ((bf16[128,2,1024]{2,1,0:T(2,128)(2,1)}), bf16[128,2,1024]{2,1,0:T(2,128)(2,1)S(1)}, u32[]{:S(2)}, u32[]{:S(2)}) async-start(bf16[128,2,1024]{2,1,0:T(2,128)(2,1)} %reshape.387), calls=%async_computation | async-start | bytes 1048576 | tf_op jit(solution)/shard_map/all_to_all | solution.py:86
  23.8 0.5 copy.65
  24.3 2.8 reshape.369
  27.2 0.9 copy.55
  28.2 3.7 reduce.10
  31.9 1.2 reshape.391
  33.0 0.6 dynamic_slice.21
  34.1 7.9 %all-to-all-done = bf16[128,2,1024]{2,1,0:T(2,128)(2,1)S(1)} async-done(((bf16[128,2,1024]{2,1,0:T(2,128)(2,1)}), bf16[128,2,1024]{2,1,0:T(2,128)(2,1)S(1)}, u32[]{:S(2)}, u32[]{:S(2)}) %all-to-all-start) | async-done | bytes 524320 | tf_op jit(solution)/shard_map/all_to_all | solution.py:86
  42.0 6.4 %all-to-all-start.2 = ((bf16[128,2,1024]{2,1,0:T(2,128)(2,1)}), bf16[128,2,1024]{2,1,0:T(2,128)(2,1)S(1)}, u32[]{:S(2)}, u32[]{:S(2)}) async-start(bf16[128,2,1024]{2,1,0:T(2,128)(2,1)} %reshape.391), calls=%async_computation.2 | async-start | bytes 1048576 | tf_op jit(solution)/shard_map/all_to_all | solution.py:85
  48.4 0.5 reshape.388
  48.9 3.0 bitcast_reduce_fusion.1
  51.9 1.1 reshape.370
  53.0 1.4 copy.49
  54.4 0.3 convolution_bitcast_fusion
  54.7 0.6 slice.220
  55.3 0.6 slice.223
  56.3 0.3 slice.228
  56.6 0.3 slice.230
  59.5 0.3 slice.226
  62.5 0.6 slice.217
  63.2 0.3 pad.74
  63.6 0.3 pad.73
  64.2 0.6 pad.75
  64.9 0.6 pad.76
  65.5 0.3 rev.5
  65.9 1.0 fusion.7
  66.9 1.7 fusion.3
  68.8 0.5 all_to_all.48
  69.4 3.7 reduce.9
  73.0 1.2 reshape.389
  74.2 12.9 %all-to-all-start.1 = ((bf16[128,2,1024]{2,1,0:T(2,128)(2,1)}), bf16[128,2,1024]{2,1,0:T(2,128)(2,1)}, u32[]{:S(2)}, u32[]{:S(2)}) async-start(bf16[128,2,1024]{2,1,0:T(2,128)(2,1)} %reshape.389), calls=%async_computation.1 | async-start | bytes 1048576 | tf_op jit(solution)/shard_map/all_to_all | solution.py:105
  87.2 0.5 reshape.392
  87.6 3.0 bitcast_reduce_fusion
  90.6 0.3 reshape.373
  90.9 0.5 fusion.11
  91.4 1.6 concatenate.49
  93.1 2.9 reshape.374
  96.0 1.5 concatenate.50
  97.5 1.7 reshape.375
  99.2 0.6 fusion.4
  100.2 289.8 %all-reduce.22 = (f32[16,16]{1,0:T(8,128)S(1)}, f32[128]{0:T(128)}) all-reduce(f32[16,16]{1,0:T(8,128)S(1)} %multiply_multiply_fusion, f32[128]{0:T(128)S(1)} %broadcast_multiply_fusion.1), channel_id=1, replica_groups=mesh['seq'=128,'chan'=2] {'seq'}, use_global_device_ids=true, to_apply=%region_2.3 | all-reduce | flops 384 | bytes 3072 | tf_op jit(solution)/shard_map/psum | solution.py:108
  390.0 7.1 %psum.22 = f32[16,16]{1,0:T(8,128)} all-reduce(f32[16,16]{1,0:T(8,128)S(1)} %get-tuple-element.29), channel_id=1, replica_groups=mesh['seq'=128,'chan'=2] {'chan'}, use_global_device_ids=true, to_apply=%region_3.4 | all-reduce | flops 256 | bytes 2048 | tf_op jit(solution)/shard_map/psum | solution.py:109
  397.1 3.6 reshape.390
  400.7 1.9 copy.54
  (102 shorter events, 8.0 us)
Async XLA Ops:
  3.1 19.8 %copy-start.3 = (f32[16,16]{1,0:T(8,128)S(1)}, f32[16,16]{1,0:T(8,128)}, u32[]{:S(2)}) copy-start(f32[16,16]{1,0:T(8,128)} %param.8) | copy-start | bytes 3076
  3.1 20.0 %copy-start.4 = (f32[16,16]{1,0:T(8,128)S(1)}, f32[16,16]{1,0:T(8,128)}, u32[]{:S(2)}) copy-start(f32[16,16]{1,0:T(8,128)} %param.7) | copy-start | bytes 3076
  8.5 33.5 %all-to-all-start = ((bf16[128,2,1024]{2,1,0:T(2,128)(2,1)}), bf16[128,2,1024]{2,1,0:T(2,128)(2,1)S(1)}, u32[]{:S(2)}, u32[]{:S(2)}) async-start(bf16[128,2,1024]{2,1,0:T(2,128)(2,1)} %reshape.387), calls=%async_computation | async-start | bytes 1048576 | tf_op jit(solution)/shard_map/all_to_all | solution.py:86
  24.2 3.0 copy-start.2
  27.2 5.8 %copy-start.5 = (f32[128]{0:T(128)S(1)}, f32[128]{0:T(128)}, u32[]{:S(2)}) copy-start(f32[128]{0:T(128)} %param.9) | copy-start | bytes 1540
  27.2 6.4 %copy-start.1 = (bf16[2048,128]{1,0:T(8,128)(2,1)S(1)}, bf16[2048,128]{1,0:T(8,128)(2,1)}, u32[]{:S(2)}) copy-start(bf16[2048,128]{1,0:T(8,128)(2,1)} %param.6) | copy-start | bytes 1572868
  42.0 32.2 %all-to-all-start.2 = ((bf16[128,2,1024]{2,1,0:T(2,128)(2,1)}), bf16[128,2,1024]{2,1,0:T(2,128)(2,1)S(1)}, u32[]{:S(2)}, u32[]{:S(2)}) async-start(bf16[128,2,1024]{2,1,0:T(2,128)(2,1)} %reshape.391), calls=%async_computation.2 | async-start | bytes 1048576 | tf_op jit(solution)/shard_map/all_to_all | solution.py:85
  53.0 12.9 %copy-start = (f32[512,1023]{1,0:T(8,128)S(1)}, f32[512,1023]{1,0:T(8,128)}, u32[]{:S(2)}) copy-start(f32[512,1023]{1,0:T(8,128)} %reshape.369) | copy-start | bytes 6285316
  74.2 322.9 %all-to-all-start.1 = ((bf16[128,2,1024]{2,1,0:T(2,128)(2,1)}), bf16[128,2,1024]{2,1,0:T(2,128)(2,1)}, u32[]{:S(2)}, u32[]{:S(2)}) async-start(bf16[128,2,1024]{2,1,0:T(2,128)(2,1)} %reshape.389), calls=%async_computation.1 | async-start | bytes 1048576 | tf_op jit(solution)/shard_map/all_to_all | solution.py:105
where the time goes:
time: 408 us; the launch traced here: 403 us
  blocking collectives  297 us (73%)
  local copies, waits for them, and re-layouts  44.4 us (11%)
  starting transfers between devices  33.8 us (8%)
  other arithmetic  13.7 us (3%)
  waiting for transfers between devices  7.9 us (2%)
  matrix products  4.83 us (1%)
    psum x1, blocking collectives, shards(): group_grad, skip_grad = lax.psum((group_grad, skip_partial), 'seq')  290 us
    all_to_all x1, starting transfers between devices, shards(): lax.all_to_all(cotangent, 'seq', split_axis=1, concat_axis=0, tiled=True)  14.4 us
    all_to_all x1, starting transfers between devices, shards(): lax.all_to_all(dx_wide, 'seq', split_axis=0, concat_axis=1, tiled=True)  12.9 us
    unnamed x3, other arithmetic  11 us
    unnamed x22, local copies, waits for them, and re-layouts  9.43 us
  transfers between devices with their start and end apart: 3, of which 1 were waited for; matrix products, arithmetic and copies ran while one was open for 12% of the time, Pallas kernels for 0%

commit v1 on v0

--- a/solution.py
+++ b/solution.py
@@ -81,9 +81,19 @@
     skip_partial = jnp.einsum(
         "tc,tc->c", inputs, cotangent, preferred_element_type=jnp.float32
     ) / math.sqrt(total_len)
+
+    def _measure_corner(d_out, matrix, device_axis, join_dim):
+        long_array = jnp.concatenate(
+            jax.lax.all_to_all(
+                jnp.stack(jnp.split(matrix, jax.lax.psum(1, device_axis), d_out)), device_axis, 0, 0
+            ),
+            join_dim,
+        )
+        return long_array
+
     x_wide, y_wide = (
         lax.all_to_all(inputs, "seq", split_axis=1, concat_axis=0, tiled=True),
-        lax.all_to_all(cotangent, "seq", split_axis=1, concat_axis=0, tiled=True),
+        _measure_corner(1, cotangent, "seq", join_dim=0),
     )
     chan_dev = x_wide.shape[1]
     full_blocks = total_len // BLOCK

time: 408 us -> 453 us (1.11)
  local copies, waits for them, and re-layouts: 44.4 us -> 91.3 us
    split x0 -> x7, local copies, waits for them, and re-layouts: none -> 45.7 us  [_measure_corner(): jnp.split(matrix, jax.lax.psum(1, device_axis), d_out)]
    unnamed x22 -> x150, local copies, waits for them, and re-layouts: 9.43 us -> 11.5 us
  transfers between devices with their start and end apart: 3 -> 3, of which waited for: 1 -> 1; matrix products, arithmetic and copies ran while one was open for 12% -> 11% of each run, Pallas kernels for 0% -> 0%
where the time goes in v1:
time: 453 us; the launch traced here: 449 us
  blocking collectives  297 us (66%)
  local copies, waits for them, and re-layouts  91.3 us (20%)
  starting transfers between devices  33.3 us (7%)
  other arithmetic  13.7 us (3%)
  waiting for transfers between devices  6.3 us (1%)
  matrix products  4.78 us (1%)
    psum x1, blocking collectives, shards(): group_grad, skip_grad = lax.psum((group_grad, skip_partial), 'seq')  290 us
    split x7, local copies, waits for them, and re-layouts, _measure_corner(): jnp.split(matrix, jax.lax.psum(1, device_axis), d_out)  45.7 us
    all_to_all x1, starting transfers between devices, _measure_corner(): jax.lax.all_to_all(jnp.stack(jnp.split(matrix, jax.lax.psum(1, device_axi...  14 us
    all_to_all x1, starting transfers between devices, shards(): lax.all_to_all(dx_wide, 'seq', split_axis=0, concat_axis=1, tiled=True)  12.9 us
    unnamed x150, local copies, waits for them, and re-layouts  11.5 us
    unnamed x3, other arithmetic  11 us
  transfers between devices with their start and end apart: 3, of which 1 were waited for; matrix products, arithmetic and copies ran while one was open for 11% of the time, Pallas kernels for 0%

profile of v1, /device:TPU:4, one launch (start us, length us, event | category | flops | bytes accessed | tf_op | source)
XLA Modules:
  0.0 448.5 jit_solution(13490783608067887817)
XLA Ops:
  0.6 8.9 %slice_reduce_fusion.116 = (bf16[2048]{0:T(1024)(128)(2,1)S(1)}, bf16[2048]{0:T(1024)(128)(2,1)S(1)}, bf16[2048]{0:T(1024)(128)(2,1)S(1)}, bf16[2048]{0:T(1024)(...) fusion(bf16[2048,128]{1,0:T(8,128)(2,1)} %param.6), kind=kLoop, calls=%fused_computation.140 | loop fusion | bytes 114688 | tf_op jit(solution)/shard_map/split | solution.py:88
  9.5 6.2 %slice_reduce_fusion.97 = (bf16[2048]{0:T(1024)(128)(2,1)S(1)}, bf16[2048]{0:T(1024)(128)(2,1)S(1)}, bf16[2048]{0:T(1024)(128)(2,1)S(1)}, bf16[2048]{0:T(1024)(1...) fusion(bf16[2048,128]{1,0:T(8,128)(2,1)S(1)} %copy-done), kind=kLoop, calls=%fused_computation.121 | loop fusion | bytes 155648 | tf_op jit(solution)/shard_map/split | solution.py:88
  15.8 6.0 %slice_reduce_fusion.78 = (bf16[2048]{0:T(1024)(128)(2,1)S(1)}, bf16[2048]{0:T(1024)(128)(2,1)S(1)}, bf16[2048]{0:T(1024)(128)(2,1)S(1)}, bf16[2048]{0:T(1024)(1...) fusion(bf16[2048,128]{1,0:T(8,128)(2,1)S(1)} %copy-done), kind=kLoop, calls=%fused_computation.102 | loop fusion | bytes 155648 | tf_op jit(solution)/shard_map/split | solution.py:88
  21.8 6.0 %slice_reduce_fusion.59 = (bf16[2048]{0:T(1024)(128)(2,1)S(1)}, bf16[2048]{0:T(1024)(128)(2,1)S(1)}, bf16[2048]{0:T(1024)(128)(2,1)S(1)}, bf16[2048]{0:T(1024)(1...) fusion(bf16[2048,128]{1,0:T(8,128)(2,1)S(1)} %copy-done), kind=kLoop, calls=%fused_computation.83 | loop fusion | bytes 155648 | tf_op jit(solution)/shard_map/split | solution.py:88
  27.9 6.0 %slice_reduce_fusion.40 = (bf16[2048]{0:T(1024)(128)(2,1)S(1)}, bf16[2048]{0:T(1024)(128)(2,1)S(1)}, bf16[2048]{0:T(1024)(128)(2,1)S(1)}, bf16[2048]{0:T(1024)(1...) fusion(bf16[2048,128]{1,0:T(8,128)(2,1)S(1)} %copy-done), kind=kLoop, calls=%fused_computation.64 | loop fusion | bytes 155648 | tf_op jit(solution)/shard_map/split | solution.py:88
  33.9 6.4 %slice_reduce_fusion.21 = (bf16[2048]{0:T(1024)(128)(2,1)S(1)}, bf16[2048]{0:T(1024)(128)(2,1)S(1)}, bf16[2048]{0:T(1024)(128)(2,1)S(1)}, bf16[2048]{0:T(1024)(1...) fusion(bf16[2048,128]{1,0:T(8,128)(2,1)S(1)} %copy-done), kind=kLoop, calls=%fused_computation.45 | loop fusion | bytes 155648 | tf_op jit(solution)/shard_map/split | solution.py:88
  40.4 6.0 %slice_reduce_fusion.1 = (bf16[2048]{0:T(1024)(128)(2,1)S(1)}, bf16[2048]{0:T(1024)(128)(2,1)S(1)}, bf16[2048]{0:T(1024)(128)(2,1)S(1)}, bf16[2048]{0:T(1024)(12...) fusion(bf16[2048,128]{1,0:T(8,128)(2,1)S(1)} %copy-done), kind=kLoop, calls=%fused_computation.25 | loop fusion | bytes 155648 | tf_op jit(solution)/shard_map/split | solution.py:88
  48.7 0.5 broadcast.457
  49.2 3.7 reduce.264
  52.9 1.2 reshape.508
  54.1 14.0 %all-to-all-start = ((bf16[128,2,1024]{2,1,0:T(2,128)(2,1)}), bf16[128,2,1024]{2,1,0:T(2,128)(2,1)S(1)}, u32[]{:S(2)}, u32[]{:S(2)}) async-start(bf16[128,2,1024]{2,1,0:T(2,128)(2,1)} %reshape.508), calls=%async_computation | async-start | bytes 1048576 | tf_op jit(solution)/shard_map/all_to_all | solution.py:87
  68.9 0.5 copy.75
  69.4 2.8 reshape.362
  72.3 2.5 copy.62
  74.9 3.7 reduce.266
  78.6 1.2 reshape.512
  79.8 0.6 dynamic_slice.21
  80.8 6.3 %all-to-all-done = bf16[128,2,1024]{2,1,0:T(2,128)(2,1)S(1)} async-done(((bf16[128,2,1024]{2,1,0:T(2,128)(2,1)}), bf16[128,2,1024]{2,1,0:T(2,128)(2,1)S(1)}, u32[]{:S(2)}, u32[]{:S(2)}) %all-to-all-start) | async-done | bytes 524320 | tf_op jit(solution)/shard_map/all_to_all | solution.py:87
  87.1 6.4 %all-to-all-start.2 = ((bf16[128,2,1024]{2,1,0:T(2,128)(2,1)}), bf16[128,2,1024]{2,1,0:T(2,128)(2,1)S(1)}, u32[]{:S(2)}, u32[]{:S(2)}) async-start(bf16[128,2,1024]{2,1,0:T(2,128)(2,1)} %reshape.512), calls=%async_computation.2 | async-start | bytes 1048576 | tf_op jit(solution)/shard_map/all_to_all | solution.py:95
  93.6 0.5 reshape.509
  94.0 3.0 bitcast_reduce_fusion.1
  97.0 1.1 reshape_reshape.3
  98.1 1.4 copy.56
  99.9 0.6 slice.220
  100.5 0.6 slice.223
  101.5 0.3 slice.228
  101.8 0.3 slice.230
  107.7 0.6 slice.217
  109.4 0.6 pad.75
  110.0 0.6 pad.76
  111.0 1.0 fusion.7
  112.0 1.7 fusion.3
  114.0 0.6 all_to_all.37
  114.6 3.7 reduce.265
  118.2 1.2 reshape.510
  119.4 12.9 %all-to-all-start.1 = ((bf16[128,2,1024]{2,1,0:T(2,128)(2,1)}), bf16[128,2,1024]{2,1,0:T(2,128)(2,1)}, u32[]{:S(2)}, u32[]{:S(2)}) async-start(bf16[128,2,1024]{2,1,0:T(2,128)(2,1)} %reshape.510), calls=%async_computation.1 | async-start | bytes 1048576 | tf_op jit(solution)/shard_map/all_to_all | solution.py:115
  132.4 0.5 reshape.513
  132.8 3.0 bitcast_reduce_fusion
  136.2 0.4 convolution_bitcast_fusion
  136.9 1.6 concatenate.49.clone
  138.6 2.9 reshape.366
  141.5 1.5 concatenate.50
  143.0 1.7 reshape.367
  144.7 0.6 fusion.4
  145.7 289.8 %all-reduce.22 = (f32[16,16]{1,0:T(8,128)S(1)}, f32[128]{0:T(128)}) all-reduce(f32[16,16]{1,0:T(8,128)S(1)} %multiply_multiply_fusion, f32[128]{0:T(128)S(1)} %broadcast_multiply_fusion.1), channel_id=1, replica_groups=mesh['seq'=128,'chan'=2] {'seq'}, use_global_device_ids=true, to_apply=%region_2.3 | all-reduce | flops 384 | bytes 3072 | tf_op jit(solution)/shard_map/psum | solution.py:118
  435.5 7.1 %psum.22 = f32[16,16]{1,0:T(8,128)} all-reduce(f32[16,16]{1,0:T(8,128)S(1)} %get-tuple-element.169), channel_id=1, replica_groups=mesh['seq'=128,'chan'=2] {'chan'}, use_global_device_ids=true, to_apply=%region_3.4 | all-reduce | flops 256 | bytes 2048 | tf_op jit(solution)/shard_map/psum | solution.py:119
  442.6 3.6 reshape.511
  446.2 1.9 copy.61
  (237 shorter events, 12.0 us)
Async XLA Ops:
  0.6 8.9 %copy-start = (bf16[2048,128]{1,0:T(8,128)(2,1)S(1)}, bf16[2048,128]{1,0:T(8,128)(2,1)}, u32[]{:S(2)}) copy-start(bf16[2048,128]{1,0:T(8,128)(2,1)} %param.6) | copy-start | bytes 1572868
  48.1 20.0 %copy-start.3 = (f32[16,16]{1,0:T(8,128)S(1)}, f32[16,16]{1,0:T(8,128)}, u32[]{:S(2)}) copy-start(f32[16,16]{1,0:T(8,128)} %param.8) | copy-start | bytes 3076
  48.1 20.1 %copy-start.4 = (f32[16,16]{1,0:T(8,128)S(1)}, f32[16,16]{1,0:T(8,128)}, u32[]{:S(2)}) copy-start(f32[16,16]{1,0:T(8,128)} %param.7) | copy-start | bytes 3076
  54.1 33.0 %all-to-all-start = ((bf16[128,2,1024]{2,1,0:T(2,128)(2,1)}), bf16[128,2,1024]{2,1,0:T(2,128)(2,1)S(1)}, u32[]{:S(2)}, u32[]{:S(2)}) async-start(bf16[128,2,1024]{2,1,0:T(2,128)(2,1)} %reshape.508), calls=%async_computation | async-start | bytes 1048576 | tf_op jit(solution)/shard_map/all_to_all | solution.py:87
  72.3 7.4 %copy-start.5 = (f32[128]{0:T(128)S(1)}, f32[128]{0:T(128)}, u32[]{:S(2)}) copy-start(f32[128]{0:T(128)} %param.9) | copy-start | bytes 1540
  72.3 8.0 %copy-start.2 = (bf16[2048,128]{1,0:T(8,128)(2,1)S(1)}, bf16[2048,128]{1,0:T(8,128)(2,1)}, u32[]{:S(2)}) copy-start(bf16[2048,128]{1,0:T(8,128)(2,1)} %param.5) | copy-start | bytes 1572868
  87.1 32.3 %all-to-all-start.2 = ((bf16[128,2,1024]{2,1,0:T(2,128)(2,1)}), bf16[128,2,1024]{2,1,0:T(2,128)(2,1)S(1)}, u32[]{:S(2)}, u32[]{:S(2)}) async-start(bf16[128,2,1024]{2,1,0:T(2,128)(2,1)} %reshape.512), calls=%async_computation.2 | async-start | bytes 1048576 | tf_op jit(solution)/shard_map/all_to_all | solution.py:95
  98.1 12.9 %copy-start.1 = (f32[512,1023]{1,0:T(8,128)S(1)}, f32[512,1023]{1,0:T(8,128)}, u32[]{:S(2)}) copy-start(f32[512,1023]{1,0:T(8,128)} %reshape.362) | copy-start | bytes 6285316
  119.4 323.2 %all-to-all-start.1 = ((bf16[128,2,1024]{2,1,0:T(2,128)(2,1)}), bf16[128,2,1024]{2,1,0:T(2,128)(2,1)}, u32[]{:S(2)}, u32[]{:S(2)}) async-start(bf16[128,2,1024]{2,1,0:T(2,128)(2,1)} %reshape.510), calls=%async_computation.1 | async-start | bytes 1048576 | tf_op jit(solution)/shard_map/all_to_all | solution.py:115
